TPU v7x, 128 devices: a whole 4x4x4 slice. The times are simulated.
128 devices in a mesh: exp: 16 (over z_lo, y, core), fsdp: 8 (over z_hi, x).
Axes of the slice: x: 4, y: 4, z: 4 (z_hi: 2, z_lo: 2; z = z_hi * 2 + z_lo), core: 2. Of those that a mesh axis runs over, the one named last changes fastest.
Arguments:
- tokens: bfloat16 [512, 7168], P(('exp', 'fsdp')), may hold values from -6 to 6
- expert_ids: int32 [512, 8], P(('exp', 'fsdp')), may hold values from 0 to 31, all different within a row; in each aligned block of 4 rows (0 to 3, 4 to 7, ...) at most 2 rows name the same one
- combine_weight: float32 [512, 8], P(('exp', 'fsdp')), may hold values from 0.1 to 1
- gate_weight: bfloat16 [32, 7168, 2048], P('exp', 'fsdp'), may hold values from -0.0625 to 0.0625
- up_weight: bfloat16 [32, 7168, 2048], P('exp', 'fsdp'), may hold values from -0.0625 to 0.0625
- down_weight: bfloat16 [32, 7168, 2048], P('exp', 'fsdp'), may hold values from -0.125 to 0.125
Outputs:
- mixed: bfloat16 [512, 7168], P(('exp', 'fsdp'))
Inputs may be any that keep to these rules, and one draw needn't show every extreme that they name: `expert_ids`: each row names 8 different experts. Among the 4 rows of one device no expert is named more than 2 times, a bound that some block reaches.
All inputs are finite; a program needn't handle non-finite values.
Results may differ from a plain program's by a relative error of at most 0.025.
Values may be sent and summed in bfloat16 or wider, within the bound.
No kernel may reach another device: no remote copies, remote signals or barrier semaphores. Data moves between devices by JAX's collectives and lax.ppermute only.
A program may use at most 192 MiB of HBM per device.

v0:
```python
import jax
import jax.numpy as jnp
from jax import lax
from jax.experimental import pallas as pl
from jax.experimental.pallas import tpu as pltpu
from jax.sharding import PartitionSpec as P

ROUTE_SCALE = 2.827
META = 128
UNIT = 128
RING = 4
BOTH = ("exp", "fsdp")


def params(mib):
    return pltpu.CompilerParams(vmem_limit_bytes=mib * 1024 * 1024)


def dot(a, b, dims):
    return lax.dot_general(a, b, (dims, ((), ())), preferred_element_type=jnp.float32)


def pack_rows(tokens, expert_ids, combine_weight, exp_count, fsdp_count, experts):
    rows, width = tokens.shape
    depth = width // fsdp_count

    def body(tokens_hbm, ids_hbm, weight_hbm, out_ref, tokens_ref, ids_ref, weight_ref, sems):
        moves = [
            pltpu.make_async_copy(source, target, sems.at[index])
            for index, (source, target) in enumerate(
                ((ids_hbm, ids_ref), (weight_hbm, weight_ref), (tokens_hbm, tokens_ref))
            )
        ]
        for move in moves:
            move.start()
        for move in moves:
            move.wait()
        ids, weight = ids_ref[...], weight_ref[...]
        gates = ROUTE_SCALE * weight / jnp.sum(weight, axis=1, keepdims=True)
        column = lax.broadcasted_iota(jnp.int32, (rows, META), 1)
        hits = jnp.zeros((rows, META), jnp.float32)
        high_low = jnp.zeros((rows, META), jnp.float32)
        for k in range(ids.shape[1]):
            named, gate = ids[:, k : k + 1], gates[:, k : k + 1]
            high = gate.astype(jnp.bfloat16).astype(jnp.float32)
            hits = jnp.where(column == named, 1.0, hits)
            high_low = jnp.where(column == named + experts, high, high_low)
            high_low = jnp.where(column == named + 2 * experts, gate - high, high_low)
        meta = jnp.where(column < experts, hits, high_low).astype(jnp.bfloat16)
        for f in range(fsdp_count):
            block = jnp.concatenate([tokens_ref[:, f * depth : (f + 1) * depth], meta], axis=1)
            for e in range(exp_count):
                out_ref[e, f] = block

    return pl.pallas_call(
        body,
        out_shape=jax.ShapeDtypeStruct((exp_count, fsdp_count, rows, depth + META), jnp.bfloat16),
        in_specs=[pl.BlockSpec(memory_space=pltpu.HBM)] * 3,
        scratch_shapes=[
            pltpu.VMEM(tokens.shape, tokens.dtype),
            pltpu.VMEM(expert_ids.shape, expert_ids.dtype),
            pltpu.VMEM(combine_weight.shape, combine_weight.dtype),
            pltpu.SemaphoreType.DMA((3,)),
        ],
        compiler_params=params(60),
    )(tokens, expert_ids, combine_weight)


def position(target, me):
    across = (target // RING + me // RING) % 2
    along = (target + 2 * RING - me) % RING
    return jnp.where(along < 2, along, 5 - along) * 2 + across


def gather_rows(me, rows_in, experts, total, slots):
    rows, depth = rows_in.shape[0], rows_in.shape[1] - META
    part = UNIT // (2 * RING)

    def body(me_ref, rows_ref, out_ref, info_ref, full_ref):
        meta = rows_ref[:, depth:]
        before = lax.broadcasted_iota(jnp.int32, (rows, rows), 1) < lax.broadcasted_iota(jnp.int32, (rows, rows), 0)
        source = lax.broadcasted_iota(jnp.int32, (META, META), 0)
        target = lax.broadcasted_iota(jnp.int32, (META, META), 1)
        wanted = target // experts * total + me_ref[1] * experts + target % experts
        chosen = ((source == wanted) & (target < 3 * experts)).astype(jnp.bfloat16)
        meta = dot(meta, chosen, ((1,), (0,)))
        rank = dot(before.astype(jnp.bfloat16), meta.astype(jnp.bfloat16), ((1,), (0,)))
        column = lax.broadcasted_iota(jnp.int32, (rows, META), 1)
        info = jnp.zeros((rows, META), jnp.float32)
        for index in range(experts):
            hit = meta[:, index : index + 1]
            slot = jnp.where(hit > 0.5, rank[:, index : index + 1], -1.0)
            gate = meta[:, experts + index : experts + index + 1] + meta[:, 2 * experts + index : 2 * experts + index + 1]
            info = jnp.where(column == index, slot, jnp.where(column == experts + index, gate, info))
            place = slot.astype(jnp.int32) == lax.broadcasted_iota(jnp.int32, (rows, slots), 1)
            value = dot(place.astype(jnp.bfloat16), rows_ref[:, :depth], ((0,), (0,))).astype(jnp.bfloat16)
            for block in range(slots // part):
                first = block * part // UNIT * UNIT + position(block % (2 * RING), me_ref[0]) * part
                out_ref[index, pl.ds(pl.multiple_of(first, part), part)] = value[block * part : (block + 1) * part]
            full_ref[index] = (jnp.sum(hit) > UNIT).astype(jnp.int32)
        info_ref[...] = info

    return pl.pallas_call(
        body,
        out_shape=(
            jax.ShapeDtypeStruct((experts, slots, depth), jnp.bfloat16),
            jax.ShapeDtypeStruct((rows, META), jnp.float32),
            jax.ShapeDtypeStruct((experts,), jnp.int32),
        ),
        out_specs=(
            pl.BlockSpec(memory_space=pltpu.VMEM),
            pl.BlockSpec(memory_space=pltpu.VMEM),
            pl.BlockSpec(memory_space=pltpu.SMEM),
        ),
        in_specs=[pl.BlockSpec(memory_space=pltpu.SMEM), pl.BlockSpec(memory_space=pltpu.VMEM)],
        compiler_params=params(32),
    )(me, rows_in)


def extra_unit(units, experts, local):
    return experts + local if units == 2 * experts else experts


def project(full, packed, weight, units, z_first, tile):
    experts, depth, width = weight.shape
    slots = packed.shape[1]
    part = UNIT // (2 * RING)

    def body(full_ref, packed_ref, weight_ref, *outs):
        column = pl.ds(pl.multiple_of(pl.program_id(0) * tile, tile), tile)
        local = pl.program_id(1)

        def put(unit, value):
            value = value.reshape(2 * RING, part, tile)
            for order in range(RING):
                if z_first:
                    sent, own, kept = outs
                    kept[order, unit, :, column] = value[2 * order]
                    if order == 0:
                        own[unit, :, column] = value[1]
                    else:
                        sent[order - 1, unit, :, column] = value[2 * order + 1]
                else:
                    outs[order][:, unit, :, column] = value[2 * order : 2 * order + 2]

        if units < 2 * experts:

            @pl.when(full_ref[local] == 0)
            def _():
                put(local, dot(packed_ref[local, :UNIT], weight_ref[0], ((1,), (0,))).astype(jnp.bfloat16))

        if units > experts:

            @pl.when(full_ref[local] != 0)
            def _():
                value = dot(packed_ref[local], weight_ref[0], ((1,), (0,))).astype(jnp.bfloat16)
                put(local, value[:UNIT])
                put(extra_unit(units, experts, local), value[UNIT:])

    block = (units, part, width)
    shapes = [(RING - 1,) + block, block, (RING,) + block] if z_first else [(2,) + block] * RING
    return pl.pallas_call(
        body,
        grid=(width // tile, experts),
        out_shape=tuple(jax.ShapeDtypeStruct(shape, jnp.bfloat16) for shape in shapes),
        in_specs=[
            pl.BlockSpec(memory_space=pltpu.SMEM),
            pl.BlockSpec(memory_space=pltpu.VMEM),
            pl.BlockSpec((1, depth, tile), lambda n, e: (e, 0, n)),
        ],
        out_specs=tuple(pl.BlockSpec(memory_space=pltpu.VMEM) for _ in shapes),
        compiler_params=params(32),
        cost_estimate=pl.CostEstimate(
            flops=2 * units * UNIT * depth * width,
            bytes_accessed=2 * experts * depth * width + 2 * units * UNIT * width,
            transcendentals=0,
        ),
    )(full, packed, weight)


def in_pieces(shape, piece, body):
    units, _, width = shape

    def step(index, carry):
        body(index // (width // piece), pl.ds(pl.multiple_of(index % (width // piece) * piece, piece), piece))
        return carry

    lax.fori_loop(0, units * (width // piece), step, 0)


def whole_call(body, shapes, *operands):
    return pl.pallas_call(
        body,
        out_shape=tuple(jax.ShapeDtypeStruct(shape, kind) for shape, kind in shapes),
        in_specs=[pl.BlockSpec(memory_space=pltpu.VMEM)] * len(operands),
        out_specs=tuple(pl.BlockSpec(memory_space=pltpu.VMEM) for _ in shapes),
        compiler_params=params(32),
    )(*operands)


def wide(value):
    return value.astype(jnp.float32)


def fold(kept, came):
    block = kept.shape[1:]

    def body(kept_ref, came_ref, *outs):
        for order, out_ref in enumerate(outs):

            def piece(unit, column):
                total = wide(kept_ref[order + 1, unit, :, column]) + wide(came_ref[order, unit, :, column])
                out_ref[unit, :, column] = total.astype(jnp.bfloat16)

            in_pieces(block, 512, piece)

    return whole_call(body, [(block, jnp.bfloat16)] * (RING - 1), kept, came)


def add_along(*terms):
    block = terms[0].shape[1:]

    def body(*refs):
        for side, out_ref in ((1, refs[-2]), (0, refs[-1])):

            def piece(unit, column):
                total = sum(wide(ref[side, unit, :, column]) for ref in refs[1:-2])
                out_ref[unit, :, column] = (total + wide(refs[0][side, unit, :, column])).astype(out_ref.dtype)

            in_pieces(block, 512, piece)

    return whole_call(body, [(block, jnp.bfloat16), (block, jnp.float32)], *terms)


def activate(stays, came, kept, *terms):
    block = stays.shape

    def body(stays_ref, came_ref, kept_ref, *refs):
        def piece(unit, column):
            gate = stays_ref[unit, :, column] + wide(came_ref[unit, :, column])
            up = sum(wide(ref[unit, :, column]) for ref in refs[:-1]) + wide(kept_ref[0, unit, :, column])
            refs[-1][unit, :, column] = (gate / (1.0 + jnp.exp(-gate)) * up).astype(jnp.bfloat16)

        in_pieces(block, 512, piece)

    return whole_call(body, [(block, jnp.bfloat16)], stays, came, kept, *terms)[0]


def along(value, step):
    return lax.ppermute(value, "fsdp", [(i, i // RING * RING + (i + step) % RING) for i in range(2 * RING)])


def across(value):
    return lax.ppermute(value, "fsdp", [(i, (i + RING) % (2 * RING)) for i in range(2 * RING)])


def to_others(right, left, far):
    return along(right, 1), along(left, -1), along(far, 2)


def finish(full, me, info, parts, down_weight, tile):
    units, part, width = parts[0].shape
    experts, features = down_weight.shape[:2]
    rows = info.shape[0]
    count = len(parts)

    def body(full_ref, me_ref, info_ref, *refs):
        part_refs, (down_ref, out_ref, hidden, total, mixed) = refs[:count], refs[count:]
        local = pl.program_id(0)

        @pl.when(local == 0)
        def _():
            mixed[...] = jnp.zeros_like(mixed)

        def put(slots):
            for index, ref in enumerate(part_refs):
                order, side = index // 2, index % 2
                step = (0, 1, RING - 1, 2)[order]
                target = (me_ref[0] // RING + side) % 2 * RING + (me_ref[0] + step) % RING
                for first in range(0, slots, UNIT):
                    unit = extra_unit(units, experts, local) if first else local
                    hidden[pl.ds(pl.multiple_of(target * part + first, part), part)] = ref[unit]

            def step(index, carry):
                chosen = pl.ds(pl.multiple_of(index * tile, tile), tile)
                value = dot(down_ref[local, chosen], hidden[:slots], ((1,), (1,)))
                total[chosen, :slots] = value.astype(jnp.bfloat16)
                return carry

            lax.fori_loop(0, features // tile, step, 0)
            slot = jnp.where(local == 0, info_ref[:, :1], info_ref[:, 1:2])
            gate = jnp.where(local == 0, info_ref[:, 2:3], info_ref[:, 3:4])
            place = slot.astype(jnp.int32) == lax.broadcasted_iota(jnp.int32, (rows, slots), 1)
            mixed[...] += dot(place.astype(jnp.bfloat16), total[:, :slots], ((1,), (1,))) * gate

        if units < 2 * experts:

            @pl.when(full_ref[local] == 0)
            def _():
                put(UNIT)

        if units > experts:

            @pl.when(full_ref[local] != 0)
            def _():
                put(2 * UNIT)

        @pl.when(local == experts - 1)
        def _():
            out_ref[...] = mixed[...].astype(jnp.bfloat16)

    scalars, whole = pl.BlockSpec(memory_space=pltpu.SMEM), pl.BlockSpec(memory_space=pltpu.VMEM)
    return pl.pallas_call(
        body,
        grid=(experts,),
        out_shape=jax.ShapeDtypeStruct((rows, features), jnp.bfloat16),
        in_specs=[scalars, scalars] + [whole] * (count + 2),
        out_specs=whole,
        scratch_shapes=[
            pltpu.VMEM((2 * UNIT, width), jnp.bfloat16),
            pltpu.VMEM((features, 2 * UNIT), jnp.bfloat16),
            pltpu.VMEM((rows, features), jnp.float32),
        ],
        compiler_params=params(24),
        cost_estimate=pl.CostEstimate(
            flops=2 * units * UNIT * features * width,
            bytes_accessed=2 * experts * features * width + 2 * units * UNIT * width,
            transcendentals=0,
        ),
    )(full, me, info, *parts, down_weight)


def on_device(tokens, expert_ids, combine_weight, gate_weight, up_weight, down_weight):
    exp_count, fsdp_count = lax.axis_size("exp"), lax.axis_size("fsdp")
    devices = exp_count * fsdp_count
    rows_dev, width = tokens.shape
    experts, depth, _ = gate_weight.shape
    sent = pack_rows(tokens, expert_ids, combine_weight, exp_count, fsdp_count, exp_count * experts)
    sent = sent.reshape((devices,) + sent.shape[2:])
    rows_in = lax.all_to_all(sent, BOTH, 0, 0, tiled=True).reshape(devices * rows_dev, depth + META)
    me = jnp.stack([lax.axis_index("fsdp"), lax.axis_index("exp")]).astype(jnp.int32)
    packed, info, full = gather_rows(me, rows_in, experts, exp_count * experts, 2 * UNIT)

    def routed(units, full, packed, info, gate_weight, up_weight, down_weight):
        sent, own, kept = project(full, packed, up_weight, units, True, 2048)
        packed, sent = lax.optimization_barrier((packed, sent))
        gate_kept, *gate_terms = project(full, packed, gate_weight, units, False, 2048)
        came = across(sent)
        own = across(own)
        gate_terms = to_others(*gate_terms)
        up_terms = fold(kept, came)
        gate_kept, up_terms = lax.optimization_barrier((gate_kept, up_terms))
        up_terms = to_others(*up_terms)
        sent, stays = add_along(gate_kept, *gate_terms)
        hidden = activate(stays, across(sent), kept, own, *up_terms)
        other = across(hidden)
        right, left, far = along(hidden, -1), along(hidden, 1), along(hidden, 2)
        right_other, left_other, far_other = along(other, -1), along(other, 1), across(far)
        parts = hidden, other, right, right_other, left, left_other, far, far_other
        return finish(full, me, info, parts, down_weight, 448)

    order = (experts + 1, 2 * experts, experts)
    branches = [lambda *operands, units=units: routed(units, *operands) for units in order]
    number = (jnp.sum(full) + len(order) - 1) % len(order)
    mixed = lax.switch(number, branches, full, packed, info, gate_weight, up_weight, down_weight)
    home = lax.all_to_all(mixed.reshape(devices, rows_dev, depth), BOTH, 0, 0, tiled=True)
    home = home.reshape(exp_count, fsdp_count, rows_dev, depth).astype(jnp.float32)
    return jnp.sum(home, axis=0).astype(jnp.bfloat16).transpose(1, 0, 2).reshape(rows_dev, width)


def solution(mesh):
    return jax.shard_map(
        on_device,
        mesh=mesh,
        in_specs=(
            P(BOTH, None),
            P(BOTH, None),
            P(BOTH, None),
            P("exp", "fsdp", None),
            P("exp", "fsdp", None),
            P("exp", "fsdp", None),
        ),
        out_specs=P(BOTH, None),
        check_vma=False,
    )
```

profile of v0, /device:TPU:1, one launch (start us, length us, event | category | flops | bytes accessed | tf_op | source)
XLA Modules:
  0.0 119.3 jit_solution(17181843060752656927)
XLA Ops:
  0.0 2.1 %shard_map.64 = bf16[16,8,4,1024]{3,2,1,0:T(4,128)(2,1)} custom-call(bf16[4,7168]{1,0:T(4,128)(2,1)} %tokens_hbm.1, s32[4,8]{1,0:T(4,128)} %ids_hbm.1, f32[4,8]{1,0:T(4,128)} %weight_hbm.1), custom_call_target="tpu_custom_call" | custom-call | tf_op jit(solution)/shard_map/pallas_call | solution.py:55
  2.1 11.5 %all-to-all-start = ((bf16[128,4,1024]{2,1,0:T(4,128)(2,1)}), bf16[128,4,1024]{2,1,0:T(4,128)(2,1)S(1)}, u32[]{:S(2)}, u32[]{:S(2)}) async-start(bf16[128,4,1024]{2,1,0:T(4,128)(2,1)} %bitcast.13), calls=%async_computation | async-start | bytes 2097152 | tf_op jit(solution)/shard_map/all_to_all | solution.py:340
  13.7 17.9 %all-to-all-done = bf16[128,4,1024]{2,1,0:T(4,128)(2,1)S(1)} async-done(((bf16[128,4,1024]{2,1,0:T(4,128)(2,1)}), bf16[128,4,1024]{2,1,0:T(4,128)(2,1)S(1)}, u32[]{:S(2)}, u32[]{:S(2)}) %all-to-all-start) | async-done | bytes 1048608 | tf_op jit(solution)/shard_map/all_to_all | solution.py:340
  31.9 2.5 %shard_map.65 = (bf16[2,256,896]{2,1,0:T(8,128)(2,1)S(1)}, f32[512,128]{1,0:T(8,128)S(1)}, s32[2]{0:T(128)S(1)}) custom-call(s32[2]{0:T(128)S(1)} %pad_add_fusion.me_ref, bf16[512,1024]{1,0:T(8,128)(2,1)S(1)} %reshape.16.rows_ref), custom_call_target="tpu_custom_call" | custom-call | tf_op jit(solution)/shard_map/pallas_call | solution.py:103
  34.5 0.6 reduce_sum.21
  35.8 52.4 %conditional.1 = (bf16[512,896]{1,0:T(8,128)(2,1)S(1)}) conditional(s32[]{:T(128)} %clamp.3, (s32[2]{0:T(128)S(1)}, bf16[2,256,896]{2,1,0:T(8,128)(2,1)S(1)}, bf16[2,896,2048]{2,1,0:T(8,128)(2,1)}, bf16[2,896,2048]{2,1,0:T(8,128)(2,1)}, s32[2]{0:T(128)S(1)}, /*index=5*/f32[512,128]{1,0:T(8,128)S(1)}, ...), branch_computations={%region_1.2_spmd, %region_2.3_spmd, %region_3.4_spmd} | conditional | flops 5637144576 | bytes 101712592 | solution.py:365
  36.0 4.1 %branch_2_fun.6 = (bf16[3,2,16,2048]{3,2,1,0:T(8,128)(2,1)S(1)}, bf16[2,16,2048]{2,1,0:T(8,128)(2,1)S(1)}, bf16[4,2,16,2048]{3,2,1,0:T(8,128)(2,1)S(1)}) custom-call(s32[2]{0:T(128)S(1)} %get-tuple-element.101.full_ref, bf16[2,256,896]{2,1,0:T(8,128)(2,1)S(1)} %get-tuple-element.107.packed_ref, bf16[2,896,2048]{2,1,0:T(8,128)(2,1)} %get-tuple-element.105.weight_ref), custom_call_target="tpu_custom_call" | custom-call | flops 939524096 | bytes 8388608 | tf_op jit(solution)/shard_map/cond/branch_2_fun/pallas_call | solution.py:162
  40.1 1.9 %collective-permute-start.32 = (bf16[3,2,16,2048]{3,2,1,0:T(8,128)(2,1)S(1)}, bf16[3,2,16,2048]{3,2,1,0:T(8,128)(2,1)S(1)}, u32[]{:S(2)}, u32[]{:S(2)}) collective-permute-start(bf16[3,2,16,2048]{3,2,1,0:T(8,128)(2,1)S(1)} %get-tuple-element.111), channel_id=1, source_target_pairs={{0,4},{1,5},{2,6},{3,7},{4,0},{5,1},{6,2},{7,3},{8,12},{9,13},{10,... | collective-permute-start | bytes 1179656 | tf_op jit(solution)/shard_map/cond/branch_2_fun/ppermute | solution.py:254
  42.0 2.0 %branch_2_fun.7 = (bf16[2,2,16,2048]{3,2,1,0:T(8,128)(2,1)S(1)}, bf16[2,2,16,2048]{3,2,1,0:T(8,128)(2,1)S(1)}, bf16[2,2,16,2048]{3,2,1,0:T(8,128)(2,1)S(1)}, bf16[2,2,16,2048]{3,2,1,0:T(8,128)(2,1)S(1)}) custom-call(s32[2]{0:T(128)S(1)} %get-tuple-element.101.full_ref, bf16[2,256,896]{2,1,0:T(8,128)(2,1)S(1)} %get-tuple-element.107.packed_ref, ...), custom_call_target="tpu_custom_call" | custom-call | flops 939524096 | bytes 8388608 | tf_op jit(solution)/shard_map/cond/branch_2_fun/pallas_call | solution.py:162
  44.0 0.4 collective-permute-start.33
  44.4 2.4 %collective-permute-start.34 = (bf16[2,2,16,2048]{3,2,1,0:T(8,128)(2,1)S(1)}, bf16[2,2,16,2048]{3,2,1,0:T(8,128)(2,1)S(1)}, u32[]{:S(2)}, u32[]{:S(2)}) collective-permute-start(bf16[2,2,16,2048]{3,2,1,0:T(8,128)(2,1)S(1)} %get-tuple-element.117), channel_id=1, source_target_pairs={{0,3},{1,0},{2,1},{3,2},{4,7},{5,4},{6,5},{7,6},{8,11},{9,8},{10,9... | collective-permute-start | bytes 786440 | tf_op jit(solution)/shard_map/cond/branch_2_fun/ppermute | solution.py:250
  46.8 0.5 collective-permute-start.35
  47.3 1.2 collective-permute-start.37
  48.4 2.8 %collective-permute-done.32.came_ref = bf16[3,2,16,2048]{3,2,1,0:T(8,128)(2,1)S(1)} collective-permute-done((bf16[3,2,16,2048]{3,2,1,0:T(8,128)(2,1)S(1)}, bf16[3,2,16,2048]{3,2,1,0:T(8,128)(2,1)S(1)}, u32[]{:S(2)}, u32[]{:S(2)}) %collective-permute-start.32) | collective-permute-done | bytes 393248 | tf_op jit(solution)/shard_map/cond/branch_2_fun/ppermute | solution.py:254
  51.2 0.3 branch_2_fun.8
  51.6 7.9 %collective-permute-done.35.refs_3_ = bf16[2,2,16,2048]{3,2,1,0:T(8,128)(2,1)S(1)} collective-permute-done((bf16[2,2,16,2048]{3,2,1,0:T(8,128)(2,1)S(1)}, bf16[2,2,16,2048]{3,2,1,0:T(8,128)(2,1)S(1)}, u32[]{:S(2)}, u32[]{:S(2)}) %collective-permute-start.35) | collective-permute-done | bytes 262176 | tf_op jit(solution)/shard_map/cond/branch_2_fun/ppermute | solution.py:250
  59.5 0.3 branch_2_fun.9
  59.9 0.5 collective-permute-start.38
  60.4 2.3 %collective-permute-start.39 = (bf16[2,16,2048]{2,1,0:T(8,128)(2,1)S(1)}, bf16[2,16,2048]{2,1,0:T(8,128)(2,1)S(1)}, u32[]{:S(2)}, u32[]{:S(2)}) collective-permute-start(bf16[2,16,2048]{2,1,0:T(8,128)(2,1)S(1)} %get-tuple-element.123), channel_id=1, source_target_pairs={{0,3},{1,0},{2,1},{3,2},{4,7},{5,4},{6,5},{7,6},{8,11},{9,8},{10,9... | collective-permute-start | bytes 393224 | tf_op jit(solution)/shard_map/cond/branch_2_fun/ppermute | solution.py:250
  62.7 3.1 %collective-permute-done.36.came_ref = bf16[2,16,2048]{2,1,0:T(8,128)(2,1)S(1)} collective-permute-done((bf16[2,16,2048]{2,1,0:T(8,128)(2,1)S(1)}, bf16[2,16,2048]{2,1,0:T(8,128)(2,1)S(1)}, u32[]{:S(2)}, u32[]{:S(2)}) %collective-permute-start.36) | collective-permute-done | bytes 131104 | tf_op jit(solution)/shard_map/cond/branch_2_fun/ppermute | solution.py:254
  66.0 3.2 %collective-permute-done.40.refs_3_ = bf16[2,16,2048]{2,1,0:T(8,128)(2,1)S(1)} collective-permute-done((bf16[2,16,2048]{2,1,0:T(8,128)(2,1)S(1)}, bf16[2,16,2048]{2,1,0:T(8,128)(2,1)S(1)}, u32[]{:S(2)}, u32[]{:S(2)}) %collective-permute-start.40) | collective-permute-done | bytes 131104 | tf_op jit(solution)/shard_map/cond/branch_2_fun/ppermute | solution.py:250
  69.6 2.7 %collective-permute-start.41 = (bf16[2,16,2048]{2,1,0:T(8,128)(2,1)S(1)}, bf16[2,16,2048]{2,1,0:T(8,128)(2,1)S(1)}, u32[]{:S(2)}, u32[]{:S(2)}) collective-permute-start(bf16[2,16,2048]{2,1,0:T(8,128)(2,1)S(1)} %branch_2_fun.10.refs_0_), channel_id=1, source_target_pairs={{0,4},{1,5},{2,6},{3,7},{4,0},{5,1},{6,2},{7,3},{8,12},{9,13},{10,... | collective-permute-start | bytes 393224 | tf_op jit(solution)/shard_map/cond/branch_2_fun/ppermute | solution.py:254
  72.3 3.1 %collective-permute-start.44 = (bf16[2,16,2048]{2,1,0:T(8,128)(2,1)S(1)}, bf16[2,16,2048]{2,1,0:T(8,128)(2,1)S(1)}, u32[]{:S(2)}, u32[]{:S(2)}) collective-permute-start(bf16[2,16,2048]{2,1,0:T(8,128)(2,1)S(1)} %branch_2_fun.10.refs_0_), channel_id=1, source_target_pairs={{0,1},{1,2},{2,3},{3,0},{4,5},{5,6},{6,7},{7,4},{8,9},{9,10},{10,1... | collective-permute-start | bytes 393224 | tf_op jit(solution)/shard_map/cond/branch_2_fun/ppermute | solution.py:250
  75.4 1.8 %collective-permute-start.47 = (bf16[2,16,2048]{2,1,0:T(8,128)(2,1)S(1)}, bf16[2,16,2048]{2,1,0:T(8,128)(2,1)S(1)}, u32[]{:S(2)}, u32[]{:S(2)}) collective-permute-start(bf16[2,16,2048]{2,1,0:T(8,128)(2,1)S(1)} %collective-permute-done.46.refs_6_), channel_id=1, source_target_pairs={{0,4},{1,5},{2,6},{3,7},{4,0},{5,1},{6,2},{7,3},{8,12},{9,13},{10,... | collective-permute-start | bytes 393224 | tf_op jit(solution)/shard_map/cond/branch_2_fun/ppermute | solution.py:254
  77.2 0.6 collective-permute-start.45
  77.7 2.5 %collective-permute-start.43 = (bf16[2,16,2048]{2,1,0:T(8,128)(2,1)S(1)}, bf16[2,16,2048]{2,1,0:T(8,128)(2,1)S(1)}, u32[]{:S(2)}, u32[]{:S(2)}) collective-permute-start(bf16[2,16,2048]{2,1,0:T(8,128)(2,1)S(1)} %collective-permute-done.41.refs_1_), channel_id=1, source_target_pairs={{0,3},{1,0},{2,1},{3,2},{4,7},{5,4},{6,5},{7,6},{8,11},{9,8},{10,9... | collective-permute-start | bytes 393224 | tf_op jit(solution)/shard_map/cond/branch_2_fun/ppermute | solution.py:250
  80.2 0.5 collective-permute-done.47.refs_7_
  80.7 1.9 %collective-permute-done.45.refs_5_ = bf16[2,16,2048]{2,1,0:T(8,128)(2,1)S(1)} collective-permute-done((bf16[2,16,2048]{2,1,0:T(8,128)(2,1)S(1)}, bf16[2,16,2048]{2,1,0:T(8,128)(2,1)S(1)}, u32[]{:S(2)}, u32[]{:S(2)}) %collective-permute-start.45) | collective-permute-done | bytes 131104 | tf_op jit(solution)/shard_map/cond/branch_2_fun/ppermute | solution.py:250
  82.6 0.6 collective-permute-done.43.refs_3_
  83.2 4.7 %branch_2_fun.11 = bf16[512,896]{1,0:T(8,128)(2,1)S(1)} custom-call(s32[2]{0:T(128)S(1)} %get-tuple-element.101.full_ref, s32[2]{0:T(128)S(1)} %get-tuple-element.102.me_ref, f32[512,128]{1,0:T(8,128)S(1)} %get-tuple-element.103.info_ref, bf16[2,16,2048]{2,1,0:T(8,128)(2,1)S(1)} %branch_2_fun.10.refs_0_, ...), custom_call_target="tpu_custom_call" | custom-call | flops 939524096 | bytes 8388608 | tf_op jit(solution)/shard_map/cond/branch_2_fun/pallas_call | solution.py:313
  88.4 29.9 %all_to_all.10 = bf16[128,4,896]{2,1,0:T(4,128)(2,1)S(1)} all-to-all(bf16[128,4,896]{2,1,0:T(4,128)(2,1)S(1)} %reshape.17), channel_id=1, replica_groups=mesh['exp'=16,'fsdp'=8] {'exp','fsdp'}, dimensions={0} | all-to-all | bytes 1835008 | tf_op jit(solution)/shard_map/all_to_all | solution.py:366
  118.3 1.0 reduce_sum.22
  (24 shorter events, 1.3 us)
Async XLA Ops:
  2.1 29.5 %all-to-all-start = ((bf16[128,4,1024]{2,1,0:T(4,128)(2,1)}), bf16[128,4,1024]{2,1,0:T(4,128)(2,1)S(1)}, u32[]{:S(2)}, u32[]{:S(2)}) async-start(bf16[128,4,1024]{2,1,0:T(4,128)(2,1)} %bitcast.13), calls=%async_computation | async-start | bytes 2097152 | tf_op jit(solution)/shard_map/all_to_all | solution.py:340
  36.0 6.0 %copy-start.2 = (bf16[2,896,2048]{2,1,0:T(8,128)(2,1)S(1)}, bf16[2,896,2048]{2,1,0:T(8,128)(2,1)}, u32[]{:S(2)}) copy-start(bf16[2,896,2048]{2,1,0:T(8,128)(2,1)} %get-tuple-element.108.weight_ref) | copy-start | bytes 22020100 | tf_op jit(solution)/shard_map/cond
  36.0 47.2 %slice-start.4 = ((s8[7340032]{0:T(1024)(128)(4,1)}), s8[4194304]{0:T(1024)(128)(4,1)S(1)}, s32[]{:S(2)}) async-start(s8[7340032]{0:T(1024)(128)(4,1)} %bitcast.11), calls=%async_computation.6 | async-start | bytes 8388608 | tf_op jit(solution)/shard_map/cond
  40.1 11.1 %collective-permute-start.32 = (bf16[3,2,16,2048]{3,2,1,0:T(8,128)(2,1)S(1)}, bf16[3,2,16,2048]{3,2,1,0:T(8,128)(2,1)S(1)}, u32[]{:S(2)}, u32[]{:S(2)}) collective-permute-start(bf16[3,2,16,2048]{3,2,1,0:T(8,128)(2,1)S(1)} %get-tuple-element.111), channel_id=1, source_target_pairs={{0,4},{1,5},{2,6},{3,7},{4,0},{5,1},{6,2},{7,3},{8,12},{9,13},{10,... | collective-permute-start | bytes 1179656 | tf_op jit(solution)/shard_map/cond/branch_2_fun/ppermute | solution.py:254
  42.0 41.2 %slice-start.5 = ((s8[7340032]{0:T(1024)(128)(4,1)}), s8[3145728]{0:T(1024)(128)(4,1)S(1)}, s32[]{:S(2)}) async-start(s8[7340032]{0:T(1024)(128)(4,1)} %bitcast.11), calls=%async_computation.7 | async-start | bytes 6291456 | tf_op jit(solution)/shard_map/cond
  44.0 7.6 %collective-permute-start.33 = (bf16[2,2,16,2048]{3,2,1,0:T(8,128)(2,1)S(1)}, bf16[2,2,16,2048]{3,2,1,0:T(8,128)(2,1)S(1)}, u32[]{:S(2)}, u32[]{:S(2)}) collective-permute-start(bf16[2,2,16,2048]{3,2,1,0:T(8,128)(2,1)S(1)} %get-tuple-element.116), channel_id=1, source_target_pairs={{0,1},{1,2},{2,3},{3,0},{4,5},{5,6},{6,7},{7,4},{8,9},{9,10},{10,1... | collective-permute-start | bytes 786440 | tf_op jit(solution)/shard_map/cond/branch_2_fun/ppermute | solution.py:250
  44.4 7.2 %collective-permute-start.34 = (bf16[2,2,16,2048]{3,2,1,0:T(8,128)(2,1)S(1)}, bf16[2,2,16,2048]{3,2,1,0:T(8,128)(2,1)S(1)}, u32[]{:S(2)}, u32[]{:S(2)}) collective-permute-start(bf16[2,2,16,2048]{3,2,1,0:T(8,128)(2,1)S(1)} %get-tuple-element.117), channel_id=1, source_target_pairs={{0,3},{1,0},{2,1},{3,2},{4,7},{5,4},{6,5},{7,6},{8,11},{9,8},{10,9... | collective-permute-start | bytes 786440 | tf_op jit(solution)/shard_map/cond/branch_2_fun/ppermute | solution.py:250
  46.8 12.7 %collective-permute-start.35 = (bf16[2,2,16,2048]{3,2,1,0:T(8,128)(2,1)S(1)}, bf16[2,2,16,2048]{3,2,1,0:T(8,128)(2,1)S(1)}, u32[]{:S(2)}, u32[]{:S(2)}) collective-permute-start(bf16[2,2,16,2048]{3,2,1,0:T(8,128)(2,1)S(1)} %get-tuple-element.118), channel_id=1, source_target_pairs={{0,2},{1,3},{2,0},{3,1},{4,6},{5,7},{6,4},{7,5},{8,10},{9,11},{10,... | collective-permute-start | bytes 786440 | tf_op jit(solution)/shard_map/cond/branch_2_fun/ppermute | solution.py:250
  47.3 15.4 %collective-permute-start.37 = (bf16[2,16,2048]{2,1,0:T(8,128)(2,1)S(1)}, bf16[2,16,2048]{2,1,0:T(8,128)(2,1)S(1)}, u32[]{:S(2)}, u32[]{:S(2)}) collective-permute-start(bf16[2,16,2048]{2,1,0:T(8,128)(2,1)S(1)} %get-tuple-element.121), channel_id=1, source_target_pairs={{0,4},{1,5},{2,6},{3,7},{4,0},{5,1},{6,2},{7,3},{8,12},{9,13},{10,... | collective-permute-start | bytes 393224 | tf_op jit(solution)/shard_map/cond/branch_2_fun/ppermute | solution.py:254
  59.8 6.0 %collective-permute-start.36 = (bf16[2,16,2048]{2,1,0:T(8,128)(2,1)S(1)}, bf16[2,16,2048]{2,1,0:T(8,128)(2,1)S(1)}, u32[]{:S(2)}, u32[]{:S(2)}) collective-permute-start(bf16[2,16,2048]{2,1,0:T(8,128)(2,1)S(1)} %get-tuple-element.120), channel_id=1, source_target_pairs={{0,4},{1,5},{2,6},{3,7},{4,0},{5,1},{6,2},{7,3},{8,12},{9,13},{10,... | collective-permute-start | bytes 393224 | tf_op jit(solution)/shard_map/cond/branch_2_fun/ppermute | solution.py:254
  59.9 5.9 %collective-permute-start.38 = (bf16[2,16,2048]{2,1,0:T(8,128)(2,1)S(1)}, bf16[2,16,2048]{2,1,0:T(8,128)(2,1)S(1)}, u32[]{:S(2)}, u32[]{:S(2)}) collective-permute-start(bf16[2,16,2048]{2,1,0:T(8,128)(2,1)S(1)} %get-tuple-element.122), channel_id=1, source_target_pairs={{0,1},{1,2},{2,3},{3,0},{4,5},{5,6},{6,7},{7,4},{8,9},{9,10},{10,1... | collective-permute-start | bytes 393224 | tf_op jit(solution)/shard_map/cond/branch_2_fun/ppermute | solution.py:250
  60.4 5.6 %collective-permute-start.39 = (bf16[2,16,2048]{2,1,0:T(8,128)(2,1)S(1)}, bf16[2,16,2048]{2,1,0:T(8,128)(2,1)S(1)}, u32[]{:S(2)}, u32[]{:S(2)}) collective-permute-start(bf16[2,16,2048]{2,1,0:T(8,128)(2,1)S(1)} %get-tuple-element.123), channel_id=1, source_target_pairs={{0,3},{1,0},{2,1},{3,2},{4,7},{5,4},{6,5},{7,6},{8,11},{9,8},{10,9... | collective-permute-start | bytes 393224 | tf_op jit(solution)/shard_map/cond/branch_2_fun/ppermute | solution.py:250
  62.7 6.5 %collective-permute-start.40 = (bf16[2,16,2048]{2,1,0:T(8,128)(2,1)S(1)}, bf16[2,16,2048]{2,1,0:T(8,128)(2,1)S(1)}, u32[]{:S(2)}, u32[]{:S(2)}) collective-permute-start(bf16[2,16,2048]{2,1,0:T(8,128)(2,1)S(1)} %get-tuple-element.124), channel_id=1, source_target_pairs={{0,2},{1,3},{2,0},{3,1},{4,6},{5,7},{6,4},{7,5},{8,10},{9,11},{10,... | collective-permute-start | bytes 393224 | tf_op jit(solution)/shard_map/cond/branch_2_fun/ppermute | solution.py:250
  69.5 5.9 %collective-permute-start.46 = (bf16[2,16,2048]{2,1,0:T(8,128)(2,1)S(1)}, bf16[2,16,2048]{2,1,0:T(8,128)(2,1)S(1)}, u32[]{:S(2)}, u32[]{:S(2)}) collective-permute-start(bf16[2,16,2048]{2,1,0:T(8,128)(2,1)S(1)} %branch_2_fun.10.refs_0_), channel_id=1, source_target_pairs={{0,2},{1,3},{2,0},{3,1},{4,6},{5,7},{6,4},{7,5},{8,10},{9,11},{10,... | collective-permute-start | bytes 393224 | tf_op jit(solution)/shard_map/cond/branch_2_fun/ppermute | solution.py:250
  69.6 7.6 %collective-permute-start.41 = (bf16[2,16,2048]{2,1,0:T(8,128)(2,1)S(1)}, bf16[2,16,2048]{2,1,0:T(8,128)(2,1)S(1)}, u32[]{:S(2)}, u32[]{:S(2)}) collective-permute-start(bf16[2,16,2048]{2,1,0:T(8,128)(2,1)S(1)} %branch_2_fun.10.refs_0_), channel_id=1, source_target_pairs={{0,4},{1,5},{2,6},{3,7},{4,0},{5,1},{6,2},{7,3},{8,12},{9,13},{10,... | collective-permute-start | bytes 393224 | tf_op jit(solution)/shard_map/cond/branch_2_fun/ppermute | solution.py:254
  72.3 8.0 %collective-permute-start.44 = (bf16[2,16,2048]{2,1,0:T(8,128)(2,1)S(1)}, bf16[2,16,2048]{2,1,0:T(8,128)(2,1)S(1)}, u32[]{:S(2)}, u32[]{:S(2)}) collective-permute-start(bf16[2,16,2048]{2,1,0:T(8,128)(2,1)S(1)} %branch_2_fun.10.refs_0_), channel_id=1, source_target_pairs={{0,1},{1,2},{2,3},{3,0},{4,5},{5,6},{6,7},{7,4},{8,9},{9,10},{10,1... | collective-permute-start | bytes 393224 | tf_op jit(solution)/shard_map/cond/branch_2_fun/ppermute | solution.py:250
  75.3 4.9 %collective-permute-start.42 = (bf16[2,16,2048]{2,1,0:T(8,128)(2,1)S(1)}, bf16[2,16,2048]{2,1,0:T(8,128)(2,1)S(1)}, u32[]{:S(2)}, u32[]{:S(2)}) collective-permute-start(bf16[2,16,2048]{2,1,0:T(8,128)(2,1)S(1)} %branch_2_fun.10.refs_0_), channel_id=1, source_target_pairs={{0,3},{1,0},{2,1},{3,2},{4,7},{5,4},{6,5},{7,6},{8,11},{9,8},{10,9... | collective-permute-start | bytes 393224 | tf_op jit(solution)/shard_map/cond/branch_2_fun/ppermute | solution.py:250
  75.4 5.3 %collective-permute-start.47 = (bf16[2,16,2048]{2,1,0:T(8,128)(2,1)S(1)}, bf16[2,16,2048]{2,1,0:T(8,128)(2,1)S(1)}, u32[]{:S(2)}, u32[]{:S(2)}) collective-permute-start(bf16[2,16,2048]{2,1,0:T(8,128)(2,1)S(1)} %collective-permute-done.46.refs_6_), channel_id=1, source_target_pairs={{0,4},{1,5},{2,6},{3,7},{4,0},{5,1},{6,2},{7,3},{8,12},{9,13},{10,... | collective-permute-start | bytes 393224 | tf_op jit(solution)/shard_map/cond/branch_2_fun/ppermute | solution.py:254
  77.2 5.4 %collective-permute-start.45 = (bf16[2,16,2048]{2,1,0:T(8,128)(2,1)S(1)}, bf16[2,16,2048]{2,1,0:T(8,128)(2,1)S(1)}, u32[]{:S(2)}, u32[]{:S(2)}) collective-permute-start(bf16[2,16,2048]{2,1,0:T(8,128)(2,1)S(1)} %collective-permute-done.41.refs_1_), channel_id=1, source_target_pairs={{0,1},{1,2},{2,3},{3,0},{4,5},{5,6},{6,7},{7,4},{8,9},{9,10},{10,1... | collective-permute-start | bytes 393224 | tf_op jit(solution)/shard_map/cond/branch_2_fun/ppermute | solution.py:250
  77.7 5.5 %collective-permute-start.43 = (bf16[2,16,2048]{2,1,0:T(8,128)(2,1)S(1)}, bf16[2,16,2048]{2,1,0:T(8,128)(2,1)S(1)}, u32[]{:S(2)}, u32[]{:S(2)}) collective-permute-start(bf16[2,16,2048]{2,1,0:T(8,128)(2,1)S(1)} %collective-permute-done.41.refs_1_), channel_id=1, source_target_pairs={{0,3},{1,0},{2,1},{3,2},{4,7},{5,4},{6,5},{7,6},{8,11},{9,8},{10,9... | collective-permute-start | bytes 393224 | tf_op jit(solution)/shard_map/cond/branch_2_fun/ppermute | solution.py:250
where the time goes:
time: 121 us; the launch traced here: 119 us
  waiting for transfers between devices  38.2 us (32%)
  starting transfers between devices  31.3 us (26%)
  blocking collectives  29.9 us (25%)
  Pallas kernels  16.4 us (14%)
  other arithmetic  1.72 us (1%)
    all_to_all x1, blocking collectives, on_device(): lax.all_to_all(mixed.reshape(devices, rows_dev, depth), BOTH, 0, 0, tiled...  29.9 us
    all_to_all x1, waiting for transfers between devices, on_device(): lax.all_to_all(sent, BOTH, 0, 0, tiled=True)  17.9 us
    ppermute x11, waiting for transfers between devices, along(): lax.ppermute(value, 'fsdp', [(i, i // RING * RING + (i + step) % RING) fo...  13.9 us
    ppermute x11, starting transfers between devices, along(): lax.ppermute(value, 'fsdp', [(i, i // RING * RING + (i + step) % RING) fo...  12.3 us
    all_to_all x1, starting transfers between devices, on_device(): lax.all_to_all(sent, BOTH, 0, 0, tiled=True)  11.5 us
    ppermute x5, starting transfers between devices, across(): lax.ppermute(value, 'fsdp', [(i, (i + RING) % (2 * RING)) for i in range(...  7.59 us
    ppermute x5, waiting for transfers between devices, across(): lax.ppermute(value, 'fsdp', [(i, (i + RING) % (2 * RING)) for i in range(...  6.36 us
    pallas_call x2, Pallas kernels, project(): pl.pallas_call(body, grid=(width // tile, experts), out_shape=tuple((jax....  6.08 us
  transfers between devices with their start and end apart: 17, of which 9 were waited for; matrix products, arithmetic and copies ran while one was open for 0% of the time, Pallas kernels for 2%

commit v1 on v0

--- a/solution.py
+++ b/solution.py
@@ -264,13 +264,11 @@
     rows = info.shape[0]
     count = len(parts)
 
+    room = UNIT if units == experts else 2 * UNIT
+
     def body(full_ref, me_ref, info_ref, *refs):
-        part_refs, (down_ref, out_ref, hidden, total, mixed) = refs[:count], refs[count:]
+        part_refs, (down_ref, out_ref, hidden, total) = refs[:count], refs[count:]
         local = pl.program_id(0)
-
-        @pl.when(local == 0)
-        def _():
-            mixed[...] = jnp.zeros_like(mixed)
 
         def put(slots):
             for index, ref in enumerate(part_refs):
@@ -283,21 +281,28 @@
 
             def step(index, carry):
                 chosen = pl.ds(pl.multiple_of(index * tile, tile), tile)
-                value = dot(down_ref[local, chosen], hidden[:slots], ((1,), (1,)))
-                total[chosen, :slots] = value.astype(jnp.bfloat16)
+                value = dot(down_ref[local, chosen], hidden[:slots], ((1,), (1,))).astype(jnp.bfloat16)
+                for expert in range(experts):
+
+                    @pl.when(local == expert)
+                    def _():
+                        total[chosen, expert * room : expert * room + slots] = value
+
                 return carry
 
             lax.fori_loop(0, features // tile, step, 0)
-            slot = jnp.where(local == 0, info_ref[:, :1], info_ref[:, 1:2])
-            gate = jnp.where(local == 0, info_ref[:, 2:3], info_ref[:, 3:4])
-            place = slot.astype(jnp.int32) == lax.broadcasted_iota(jnp.int32, (rows, slots), 1)
-            mixed[...] += dot(place.astype(jnp.bfloat16), total[:, :slots], ((1,), (1,))) * gate
 
         if units < 2 * experts:
 
             @pl.when(full_ref[local] == 0)
             def _():
                 put(UNIT)
+                if units > experts:
+                    for expert in range(experts):
+
+                        @pl.when(local == expert)
+                        def _():
+                            total[:, expert * room + UNIT : (expert + 1) * room] = jnp.zeros((features, UNIT), jnp.bfloat16)
 
         if units > experts:
 
@@ -307,7 +312,16 @@
 
         @pl.when(local == experts - 1)
         def _():
-            out_ref[...] = mixed[...].astype(jnp.bfloat16)
+            slot = lax.broadcasted_iota(jnp.int32, (rows, room), 1)
+            high, low = [], []
+            for expert in range(experts):
+                named = info_ref[:, expert : expert + 1].astype(jnp.int32) == slot
+                gate = info_ref[:, experts + expert : experts + expert + 1]
+                rounded = gate.astype(jnp.bfloat16).astype(jnp.float32)
+                high.append(jnp.where(named, rounded, 0.0).astype(jnp.bfloat16))
+                low.append(jnp.where(named, gate - rounded, 0.0).astype(jnp.bfloat16))
+            mixed = sum(dot(jnp.concatenate(side, axis=1), total[...], ((1,), (1,))) for side in (high, low))
+            out_ref[...] = mixed.astype(jnp.bfloat16)
 
     scalars, whole = pl.BlockSpec(memory_space=pltpu.SMEM), pl.BlockSpec(memory_space=pltpu.VMEM)
     return pl.pallas_call(
@@ -318,8 +332,7 @@
         out_specs=whole,
         scratch_shapes=[
             pltpu.VMEM((2 * UNIT, width), jnp.bfloat16),
-            pltpu.VMEM((features, 2 * UNIT), jnp.bfloat16),
-            pltpu.VMEM((rows, features), jnp.float32),
+            pltpu.VMEM((features, experts * room), jnp.bfloat16),
         ],
         compiler_params=params(24),
         cost_estimate=pl.CostEstimate(

time: 121 us -> 121 us (level)
  transfers between devices with their start and end apart: 17 -> 17, of which waited for: 9 -> 10; matrix products, arithmetic and copies ran while one was open for 0% -> 0% of each run, Pallas kernels for 2% -> 2%
where the time goes in v1:
time: 121 us; the launch traced here: 119 us
  waiting for transfers between devices  38.9 us (32%)
  starting transfers between devices  30.5 us (25%)
  blocking collectives  30 us (25%)
  Pallas kernels  16 us (13%)
  other arithmetic  1.72 us (1%)
    all_to_all x1, blocking collectives, on_device(): lax.all_to_all(mixed.reshape(devices, rows_dev, depth), BOTH, 0, 0, tiled...  30 us
    all_to_all x1, waiting for transfers between devices, on_device(): lax.all_to_all(sent, BOTH, 0, 0, tiled=True)  17.9 us
    ppermute x11, waiting for transfers between devices, along(): lax.ppermute(value, 'fsdp', [(i, i // RING * RING + (i + step) % RING) fo...  14.5 us
    ppermute x11, starting transfers between devices, along(): lax.ppermute(value, 'fsdp', [(i, i // RING * RING + (i + step) % RING) fo...  12.5 us
    all_to_all x1, starting transfers between devices, on_device(): lax.all_to_all(sent, BOTH, 0, 0, tiled=True)  11.5 us
    ppermute x5, starting transfers between devices, across(): lax.ppermute(value, 'fsdp', [(i, (i + RING) % (2 * RING)) for i in range(...  6.52 us
    ppermute x5, waiting for transfers between devices, across(): lax.ppermute(value, 'fsdp', [(i, (i + RING) % (2 * RING)) for i in range(...  6.48 us
    pallas_call x2, Pallas kernels, project(): pl.pallas_call(body, grid=(width // tile, experts), out_shape=tuple((jax....  6.09 us
  transfers between devices with their start and end apart: 17, of which 10 were waited for; matrix products, arithmetic and copies ran while one was open for 0% of the time, Pallas kernels for 2%

profile of v1, /device:TPU:1, one launch (start us, length us, event | category | flops | bytes accessed | tf_op | source)
XLA Modules:
  0.0 119.0 jit_solution(16864514862758800233)
XLA Ops:
  0.0 2.1 %shard_map.64 = bf16[16,8,4,1024]{3,2,1,0:T(4,128)(2,1)} custom-call(bf16[4,7168]{1,0:T(4,128)(2,1)} %tokens_hbm.1, s32[4,8]{1,0:T(4,128)} %ids_hbm.1, f32[4,8]{1,0:T(4,128)} %weight_hbm.1), custom_call_target="tpu_custom_call" | custom-call | tf_op jit(solution)/shard_map/pallas_call | solution.py:55
  2.1 11.5 %all-to-all-start = ((bf16[128,4,1024]{2,1,0:T(4,128)(2,1)}), bf16[128,4,1024]{2,1,0:T(4,128)(2,1)S(1)}, u32[]{:S(2)}, u32[]{:S(2)}) async-start(bf16[128,4,1024]{2,1,0:T(4,128)(2,1)} %bitcast.13), calls=%async_computation | async-start | bytes 2097152 | tf_op jit(solution)/shard_map/all_to_all | solution.py:353
  13.7 17.9 %all-to-all-done = bf16[128,4,1024]{2,1,0:T(4,128)(2,1)S(1)} async-done(((bf16[128,4,1024]{2,1,0:T(4,128)(2,1)}), bf16[128,4,1024]{2,1,0:T(4,128)(2,1)S(1)}, u32[]{:S(2)}, u32[]{:S(2)}) %all-to-all-start) | async-done | bytes 1048608 | tf_op jit(solution)/shard_map/all_to_all | solution.py:353
  31.9 2.5 %shard_map.65 = (bf16[2,256,896]{2,1,0:T(8,128)(2,1)S(1)}, f32[512,128]{1,0:T(8,128)S(1)}, s32[2]{0:T(128)S(1)}) custom-call(s32[2]{0:T(128)S(1)} %pad_add_fusion.me_ref, bf16[512,1024]{1,0:T(8,128)(2,1)S(1)} %reshape.16.rows_ref), custom_call_target="tpu_custom_call" | custom-call | tf_op jit(solution)/shard_map/pallas_call | solution.py:103
  34.5 0.6 reduce_sum.21
  35.8 51.9 %conditional.1 = (bf16[512,896]{1,0:T(8,128)(2,1)S(1)}) conditional(s32[]{:T(128)} %clamp.3, (s32[2]{0:T(128)S(1)}, bf16[2,256,896]{2,1,0:T(8,128)(2,1)S(1)}, bf16[2,896,2048]{2,1,0:T(8,128)(2,1)}, bf16[2,896,2048]{2,1,0:T(8,128)(2,1)}, s32[2]{0:T(128)S(1)}, /*index=5*/f32[512,128]{1,0:T(8,128)S(1)}, ...), branch_computations={%region_1.2_spmd, %region_2.3_spmd, %region_3.4_spmd} | conditional | flops 5637144576 | bytes 101712592 | solution.py:378
  36.0 4.1 %branch_2_fun.6 = (bf16[3,2,16,2048]{3,2,1,0:T(8,128)(2,1)S(1)}, bf16[2,16,2048]{2,1,0:T(8,128)(2,1)S(1)}, bf16[4,2,16,2048]{3,2,1,0:T(8,128)(2,1)S(1)}) custom-call(s32[2]{0:T(128)S(1)} %get-tuple-element.101.full_ref, bf16[2,256,896]{2,1,0:T(8,128)(2,1)S(1)} %get-tuple-element.107.packed_ref, bf16[2,896,2048]{2,1,0:T(8,128)(2,1)} %get-tuple-element.105.weight_ref), custom_call_target="tpu_custom_call" | custom-call | flops 939524096 | bytes 8388608 | tf_op jit(solution)/shard_map/cond/branch_2_fun/pallas_call | solution.py:162
  40.1 1.9 %collective-permute-start.32 = (bf16[3,2,16,2048]{3,2,1,0:T(8,128)(2,1)S(1)}, bf16[3,2,16,2048]{3,2,1,0:T(8,128)(2,1)S(1)}, u32[]{:S(2)}, u32[]{:S(2)}) collective-permute-start(bf16[3,2,16,2048]{3,2,1,0:T(8,128)(2,1)S(1)} %get-tuple-element.111), channel_id=1, source_target_pairs={{0,4},{1,5},{2,6},{3,7},{4,0},{5,1},{6,2},{7,3},{8,12},{9,13},{10,... | collective-permute-start | bytes 1179656 | tf_op jit(solution)/shard_map/cond/branch_2_fun/ppermute | solution.py:254
  42.0 2.0 %branch_2_fun.7 = (bf16[2,2,16,2048]{3,2,1,0:T(8,128)(2,1)S(1)}, bf16[2,2,16,2048]{3,2,1,0:T(8,128)(2,1)S(1)}, bf16[2,2,16,2048]{3,2,1,0:T(8,128)(2,1)S(1)}, bf16[2,2,16,2048]{3,2,1,0:T(8,128)(2,1)S(1)}) custom-call(s32[2]{0:T(128)S(1)} %get-tuple-element.101.full_ref, bf16[2,256,896]{2,1,0:T(8,128)(2,1)S(1)} %get-tuple-element.107.packed_ref, ...), custom_call_target="tpu_custom_call" | custom-call | flops 939524096 | bytes 8388608 | tf_op jit(solution)/shard_map/cond/branch_2_fun/pallas_call | solution.py:162
  44.0 0.4 collective-permute-start.33
  44.4 2.4 %collective-permute-start.34 = (bf16[2,2,16,2048]{3,2,1,0:T(8,128)(2,1)S(1)}, bf16[2,2,16,2048]{3,2,1,0:T(8,128)(2,1)S(1)}, u32[]{:S(2)}, u32[]{:S(2)}) collective-permute-start(bf16[2,2,16,2048]{3,2,1,0:T(8,128)(2,1)S(1)} %get-tuple-element.117), channel_id=1, source_target_pairs={{0,3},{1,0},{2,1},{3,2},{4,7},{5,4},{6,5},{7,6},{8,11},{9,8},{10,9... | collective-permute-start | bytes 786440 | tf_op jit(solution)/shard_map/cond/branch_2_fun/ppermute | solution.py:250
  46.7 0.5 collective-permute-start.35
  47.3 1.1 collective-permute-start.37
  48.4 2.8 %collective-permute-done.32.came_ref = bf16[3,2,16,2048]{3,2,1,0:T(8,128)(2,1)S(1)} collective-permute-done((bf16[3,2,16,2048]{3,2,1,0:T(8,128)(2,1)S(1)}, bf16[3,2,16,2048]{3,2,1,0:T(8,128)(2,1)S(1)}, u32[]{:S(2)}, u32[]{:S(2)}) %collective-permute-start.32) | collective-permute-done | bytes 393248 | tf_op jit(solution)/shard_map/cond/branch_2_fun/ppermute | solution.py:254
  51.2 0.3 branch_2_fun.8
  51.6 7.9 %collective-permute-done.35.refs_3_ = bf16[2,2,16,2048]{3,2,1,0:T(8,128)(2,1)S(1)} collective-permute-done((bf16[2,2,16,2048]{3,2,1,0:T(8,128)(2,1)S(1)}, bf16[2,2,16,2048]{3,2,1,0:T(8,128)(2,1)S(1)}, u32[]{:S(2)}, u32[]{:S(2)}) %collective-permute-start.35) | collective-permute-done | bytes 262176 | tf_op jit(solution)/shard_map/cond/branch_2_fun/ppermute | solution.py:250
  59.9 0.4 collective-permute-start.38
  60.3 2.6 %collective-permute-start.39 = (bf16[2,16,2048]{2,1,0:T(8,128)(2,1)S(1)}, bf16[2,16,2048]{2,1,0:T(8,128)(2,1)S(1)}, u32[]{:S(2)}, u32[]{:S(2)}) collective-permute-start(bf16[2,16,2048]{2,1,0:T(8,128)(2,1)S(1)} %get-tuple-element.123), channel_id=1, source_target_pairs={{0,3},{1,0},{2,1},{3,2},{4,7},{5,4},{6,5},{7,6},{8,11},{9,8},{10,9... | collective-permute-start | bytes 393224 | tf_op jit(solution)/shard_map/cond/branch_2_fun/ppermute | solution.py:250
  62.8 2.9 %collective-permute-done.36.came_ref = bf16[2,16,2048]{2,1,0:T(8,128)(2,1)S(1)} collective-permute-done((bf16[2,16,2048]{2,1,0:T(8,128)(2,1)S(1)}, bf16[2,16,2048]{2,1,0:T(8,128)(2,1)S(1)}, u32[]{:S(2)}, u32[]{:S(2)}) %collective-permute-start.36) | collective-permute-done | bytes 131104 | tf_op jit(solution)/shard_map/cond/branch_2_fun/ppermute | solution.py:254
  65.8 0.6 collective-permute-done.39.refs_2_
  66.3 3.5 %collective-permute-done.40.refs_3_ = bf16[2,16,2048]{2,1,0:T(8,128)(2,1)S(1)} collective-permute-done((bf16[2,16,2048]{2,1,0:T(8,128)(2,1)S(1)}, bf16[2,16,2048]{2,1,0:T(8,128)(2,1)S(1)}, u32[]{:S(2)}, u32[]{:S(2)}) %collective-permute-start.40) | collective-permute-done | bytes 131104 | tf_op jit(solution)/shard_map/cond/branch_2_fun/ppermute | solution.py:250
  70.3 2.0 %collective-permute-start.41 = (bf16[2,16,2048]{2,1,0:T(8,128)(2,1)S(1)}, bf16[2,16,2048]{2,1,0:T(8,128)(2,1)S(1)}, u32[]{:S(2)}, u32[]{:S(2)}) collective-permute-start(bf16[2,16,2048]{2,1,0:T(8,128)(2,1)S(1)} %branch_2_fun.10.refs_0_), channel_id=1, source_target_pairs={{0,4},{1,5},{2,6},{3,7},{4,0},{5,1},{6,2},{7,3},{8,12},{9,13},{10,... | collective-permute-start | bytes 393224 | tf_op jit(solution)/shard_map/cond/branch_2_fun/ppermute | solution.py:254
  72.2 3.1 %collective-permute-start.44 = (bf16[2,16,2048]{2,1,0:T(8,128)(2,1)S(1)}, bf16[2,16,2048]{2,1,0:T(8,128)(2,1)S(1)}, u32[]{:S(2)}, u32[]{:S(2)}) collective-permute-start(bf16[2,16,2048]{2,1,0:T(8,128)(2,1)S(1)} %branch_2_fun.10.refs_0_), channel_id=1, source_target_pairs={{0,1},{1,2},{2,3},{3,0},{4,5},{5,6},{6,7},{7,4},{8,9},{9,10},{10,1... | collective-permute-start | bytes 393224 | tf_op jit(solution)/shard_map/cond/branch_2_fun/ppermute | solution.py:250
  75.6 1.5 %collective-permute-start.47 = (bf16[2,16,2048]{2,1,0:T(8,128)(2,1)S(1)}, bf16[2,16,2048]{2,1,0:T(8,128)(2,1)S(1)}, u32[]{:S(2)}, u32[]{:S(2)}) collective-permute-start(bf16[2,16,2048]{2,1,0:T(8,128)(2,1)S(1)} %collective-permute-done.46.refs_6_), channel_id=1, source_target_pairs={{0,4},{1,5},{2,6},{3,7},{4,0},{5,1},{6,2},{7,3},{8,12},{9,13},{10,... | collective-permute-start | bytes 393224 | tf_op jit(solution)/shard_map/cond/branch_2_fun/ppermute | solution.py:254
  77.0 0.6 collective-permute-start.45
  77.7 2.4 %collective-permute-start.43 = (bf16[2,16,2048]{2,1,0:T(8,128)(2,1)S(1)}, bf16[2,16,2048]{2,1,0:T(8,128)(2,1)S(1)}, u32[]{:S(2)}, u32[]{:S(2)}) collective-permute-start(bf16[2,16,2048]{2,1,0:T(8,128)(2,1)S(1)} %collective-permute-done.41.refs_1_), channel_id=1, source_target_pairs={{0,3},{1,0},{2,1},{3,2},{4,7},{5,4},{6,5},{7,6},{8,11},{9,8},{10,9... | collective-permute-start | bytes 393224 | tf_op jit(solution)/shard_map/cond/branch_2_fun/ppermute | solution.py:250
  80.1 0.8 collective-permute-done.47.refs_7_
  80.9 1.6 %collective-permute-done.45.refs_5_ = bf16[2,16,2048]{2,1,0:T(8,128)(2,1)S(1)} collective-permute-done((bf16[2,16,2048]{2,1,0:T(8,128)(2,1)S(1)}, bf16[2,16,2048]{2,1,0:T(8,128)(2,1)S(1)}, u32[]{:S(2)}, u32[]{:S(2)}) %collective-permute-start.45) | collective-permute-done | bytes 131104 | tf_op jit(solution)/shard_map/cond/branch_2_fun/ppermute | solution.py:250
  82.5 0.7 collective-permute-done.43.refs_3_
  83.2 4.3 %branch_2_fun.11 = bf16[512,896]{1,0:T(8,128)(2,1)S(1)} custom-call(s32[2]{0:T(128)S(1)} %get-tuple-element.101.full_ref, s32[2]{0:T(128)S(1)} %get-tuple-element.102.me_ref, f32[512,128]{1,0:T(8,128)S(1)} %get-tuple-element.103.info_ref, bf16[2,16,2048]{2,1,0:T(8,128)(2,1)S(1)} %branch_2_fun.10.refs_0_, ...), custom_call_target="tpu_custom_call" | custom-call | flops 939524096 | bytes 8388608 | tf_op jit(solution)/shard_map/cond/branch_2_fun/pallas_call | solution.py:327
  87.9 30.0 %all_to_all.10 = bf16[128,4,896]{2,1,0:T(4,128)(2,1)S(1)} all-to-all(bf16[128,4,896]{2,1,0:T(4,128)(2,1)S(1)} %reshape.17), channel_id=1, replica_groups=mesh['exp'=16,'fsdp'=8] {'exp','fsdp'}, dimensions={0} | all-to-all | bytes 1835008 | tf_op jit(solution)/shard_map/all_to_all | solution.py:379
  118.0 1.0 reduce_sum.22
  (24 shorter events, 1.6 us)
Async XLA Ops:
  2.1 29.5 %all-to-all-start = ((bf16[128,4,1024]{2,1,0:T(4,128)(2,1)}), bf16[128,4,1024]{2,1,0:T(4,128)(2,1)S(1)}, u32[]{:S(2)}, u32[]{:S(2)}) async-start(bf16[128,4,1024]{2,1,0:T(4,128)(2,1)} %bitcast.13), calls=%async_computation | async-start | bytes 2097152 | tf_op jit(solution)/shard_map/all_to_all | solution.py:353
  36.0 6.0 %copy-start.2 = (bf16[2,896,2048]{2,1,0:T(8,128)(2,1)S(1)}, bf16[2,896,2048]{2,1,0:T(8,128)(2,1)}, u32[]{:S(2)}) copy-start(bf16[2,896,2048]{2,1,0:T(8,128)(2,1)} %get-tuple-element.108.weight_ref) | copy-start | bytes 22020100 | tf_op jit(solution)/shard_map/cond
  36.0 47.2 %slice-start.4 = ((s8[7340032]{0:T(1024)(128)(4,1)}), s8[4194304]{0:T(1024)(128)(4,1)S(1)}, s32[]{:S(2)}) async-start(s8[7340032]{0:T(1024)(128)(4,1)} %bitcast.11), calls=%async_computation.6 | async-start | bytes 8388608 | tf_op jit(solution)/shard_map/cond
  40.1 11.1 %collective-permute-start.32 = (bf16[3,2,16,2048]{3,2,1,0:T(8,128)(2,1)S(1)}, bf16[3,2,16,2048]{3,2,1,0:T(8,128)(2,1)S(1)}, u32[]{:S(2)}, u32[]{:S(2)}) collective-permute-start(bf16[3,2,16,2048]{3,2,1,0:T(8,128)(2,1)S(1)} %get-tuple-element.111), channel_id=1, source_target_pairs={{0,4},{1,5},{2,6},{3,7},{4,0},{5,1},{6,2},{7,3},{8,12},{9,13},{10,... | collective-permute-start | bytes 1179656 | tf_op jit(solution)/shard_map/cond/branch_2_fun/ppermute | solution.py:254
  42.0 41.2 %slice-start.5 = ((s8[7340032]{0:T(1024)(128)(4,1)}), s8[3145728]{0:T(1024)(128)(4,1)S(1)}, s32[]{:S(2)}) async-start(s8[7340032]{0:T(1024)(128)(4,1)} %bitcast.11), calls=%async_computation.7 | async-start | bytes 6291456 | tf_op jit(solution)/shard_map/cond
  44.0 7.6 %collective-permute-start.33 = (bf16[2,2,16,2048]{3,2,1,0:T(8,128)(2,1)S(1)}, bf16[2,2,16,2048]{3,2,1,0:T(8,128)(2,1)S(1)}, u32[]{:S(2)}, u32[]{:S(2)}) collective-permute-start(bf16[2,2,16,2048]{3,2,1,0:T(8,128)(2,1)S(1)} %get-tuple-element.116), channel_id=1, source_target_pairs={{0,1},{1,2},{2,3},{3,0},{4,5},{5,6},{6,7},{7,4},{8,9},{9,10},{10,1... | collective-permute-start | bytes 786440 | tf_op jit(solution)/shard_map/cond/branch_2_fun/ppermute | solution.py:250
  44.4 7.2 %collective-permute-start.34 = (bf16[2,2,16,2048]{3,2,1,0:T(8,128)(2,1)S(1)}, bf16[2,2,16,2048]{3,2,1,0:T(8,128)(2,1)S(1)}, u32[]{:S(2)}, u32[]{:S(2)}) collective-permute-start(bf16[2,2,16,2048]{3,2,1,0:T(8,128)(2,1)S(1)} %get-tuple-element.117), channel_id=1, source_target_pairs={{0,3},{1,0},{2,1},{3,2},{4,7},{5,4},{6,5},{7,6},{8,11},{9,8},{10,9... | collective-permute-start | bytes 786440 | tf_op jit(solution)/shard_map/cond/branch_2_fun/ppermute | solution.py:250
  46.7 12.7 %collective-permute-start.35 = (bf16[2,2,16,2048]{3,2,1,0:T(8,128)(2,1)S(1)}, bf16[2,2,16,2048]{3,2,1,0:T(8,128)(2,1)S(1)}, u32[]{:S(2)}, u32[]{:S(2)}) collective-permute-start(bf16[2,2,16,2048]{3,2,1,0:T(8,128)(2,1)S(1)} %get-tuple-element.118), channel_id=1, source_target_pairs={{0,2},{1,3},{2,0},{3,1},{4,6},{5,7},{6,4},{7,5},{8,10},{9,11},{10,... | collective-permute-start | bytes 786440 | tf_op jit(solution)/shard_map/cond/branch_2_fun/ppermute | solution.py:250
  47.3 15.6 %collective-permute-start.37 = (bf16[2,16,2048]{2,1,0:T(8,128)(2,1)S(1)}, bf16[2,16,2048]{2,1,0:T(8,128)(2,1)S(1)}, u32[]{:S(2)}, u32[]{:S(2)}) collective-permute-start(bf16[2,16,2048]{2,1,0:T(8,128)(2,1)S(1)} %get-tuple-element.121), channel_id=1, source_target_pairs={{0,4},{1,5},{2,6},{3,7},{4,0},{5,1},{6,2},{7,3},{8,12},{9,13},{10,... | collective-permute-start | bytes 393224 | tf_op jit(solution)/shard_map/cond/branch_2_fun/ppermute | solution.py:254
  59.8 6.0 %collective-permute-start.36 = (bf16[2,16,2048]{2,1,0:T(8,128)(2,1)S(1)}, bf16[2,16,2048]{2,1,0:T(8,128)(2,1)S(1)}, u32[]{:S(2)}, u32[]{:S(2)}) collective-permute-start(bf16[2,16,2048]{2,1,0:T(8,128)(2,1)S(1)} %get-tuple-element.120), channel_id=1, source_target_pairs={{0,4},{1,5},{2,6},{3,7},{4,0},{5,1},{6,2},{7,3},{8,12},{9,13},{10,... | collective-permute-start | bytes 393224 | tf_op jit(solution)/shard_map/cond/branch_2_fun/ppermute | solution.py:254
  59.9 5.9 %collective-permute-start.38 = (bf16[2,16,2048]{2,1,0:T(8,128)(2,1)S(1)}, bf16[2,16,2048]{2,1,0:T(8,128)(2,1)S(1)}, u32[]{:S(2)}, u32[]{:S(2)}) collective-permute-start(bf16[2,16,2048]{2,1,0:T(8,128)(2,1)S(1)} %get-tuple-element.122), channel_id=1, source_target_pairs={{0,1},{1,2},{2,3},{3,0},{4,5},{5,6},{6,7},{7,4},{8,9},{9,10},{10,1... | collective-permute-start | bytes 393224 | tf_op jit(solution)/shard_map/cond/branch_2_fun/ppermute | solution.py:250
  60.3 6.0 %collective-permute-start.39 = (bf16[2,16,2048]{2,1,0:T(8,128)(2,1)S(1)}, bf16[2,16,2048]{2,1,0:T(8,128)(2,1)S(1)}, u32[]{:S(2)}, u32[]{:S(2)}) collective-permute-start(bf16[2,16,2048]{2,1,0:T(8,128)(2,1)S(1)} %get-tuple-element.123), channel_id=1, source_target_pairs={{0,3},{1,0},{2,1},{3,2},{4,7},{5,4},{6,5},{7,6},{8,11},{9,8},{10,9... | collective-permute-start | bytes 393224 | tf_op jit(solution)/shard_map/cond/branch_2_fun/ppermute | solution.py:250
  62.8 7.0 %collective-permute-start.40 = (bf16[2,16,2048]{2,1,0:T(8,128)(2,1)S(1)}, bf16[2,16,2048]{2,1,0:T(8,128)(2,1)S(1)}, u32[]{:S(2)}, u32[]{:S(2)}) collective-permute-start(bf16[2,16,2048]{2,1,0:T(8,128)(2,1)S(1)} %get-tuple-element.124), channel_id=1, source_target_pairs={{0,2},{1,3},{2,0},{3,1},{4,6},{5,7},{6,4},{7,5},{8,10},{9,11},{10,... | collective-permute-start | bytes 393224 | tf_op jit(solution)/shard_map/cond/branch_2_fun/ppermute | solution.py:250
  70.2 5.4 %collective-permute-start.46 = (bf16[2,16,2048]{2,1,0:T(8,128)(2,1)S(1)}, bf16[2,16,2048]{2,1,0:T(8,128)(2,1)S(1)}, u32[]{:S(2)}, u32[]{:S(2)}) collective-permute-start(bf16[2,16,2048]{2,1,0:T(8,128)(2,1)S(1)} %branch_2_fun.10.refs_0_), channel_id=1, source_target_pairs={{0,2},{1,3},{2,0},{3,1},{4,6},{5,7},{6,4},{7,5},{8,10},{9,11},{10,... | collective-permute-start | bytes 393224 | tf_op jit(solution)/shard_map/cond/branch_2_fun/ppermute | solution.py:250
  70.3 6.8 %collective-permute-start.41 = (bf16[2,16,2048]{2,1,0:T(8,128)(2,1)S(1)}, bf16[2,16,2048]{2,1,0:T(8,128)(2,1)S(1)}, u32[]{:S(2)}, u32[]{:S(2)}) collective-permute-start(bf16[2,16,2048]{2,1,0:T(8,128)(2,1)S(1)} %branch_2_fun.10.refs_0_), channel_id=1, source_target_pairs={{0,4},{1,5},{2,6},{3,7},{4,0},{5,1},{6,2},{7,3},{8,12},{9,13},{10,... | collective-permute-start | bytes 393224 | tf_op jit(solution)/shard_map/cond/branch_2_fun/ppermute | solution.py:254
  72.2 7.9 %collective-permute-start.44 = (bf16[2,16,2048]{2,1,0:T(8,128)(2,1)S(1)}, bf16[2,16,2048]{2,1,0:T(8,128)(2,1)S(1)}, u32[]{:S(2)}, u32[]{:S(2)}) collective-permute-start(bf16[2,16,2048]{2,1,0:T(8,128)(2,1)S(1)} %branch_2_fun.10.refs_0_), channel_id=1, source_target_pairs={{0,1},{1,2},{2,3},{3,0},{4,5},{5,6},{6,7},{7,4},{8,9},{9,10},{10,1... | collective-permute-start | bytes 393224 | tf_op jit(solution)/shard_map/cond/branch_2_fun/ppermute | solution.py:250
  75.3 4.8 %collective-permute-start.42 = (bf16[2,16,2048]{2,1,0:T(8,128)(2,1)S(1)}, bf16[2,16,2048]{2,1,0:T(8,128)(2,1)S(1)}, u32[]{:S(2)}, u32[]{:S(2)}) collective-permute-start(bf16[2,16,2048]{2,1,0:T(8,128)(2,1)S(1)} %branch_2_fun.10.refs_0_), channel_id=1, source_target_pairs={{0,3},{1,0},{2,1},{3,2},{4,7},{5,4},{6,5},{7,6},{8,11},{9,8},{10,9... | collective-permute-start | bytes 393224 | tf_op jit(solution)/shard_map/cond/branch_2_fun/ppermute | solution.py:250
  75.6 5.3 %collective-permute-start.47 = (bf16[2,16,2048]{2,1,0:T(8,128)(2,1)S(1)}, bf16[2,16,2048]{2,1,0:T(8,128)(2,1)S(1)}, u32[]{:S(2)}, u32[]{:S(2)}) collective-permute-start(bf16[2,16,2048]{2,1,0:T(8,128)(2,1)S(1)} %collective-permute-done.46.refs_6_), channel_id=1, source_target_pairs={{0,4},{1,5},{2,6},{3,7},{4,0},{5,1},{6,2},{7,3},{8,12},{9,13},{10,... | collective-permute-start | bytes 393224 | tf_op jit(solution)/shard_map/cond/branch_2_fun/ppermute | solution.py:254
  77.0 5.4 %collective-permute-start.45 = (bf16[2,16,2048]{2,1,0:T(8,128)(2,1)S(1)}, bf16[2,16,2048]{2,1,0:T(8,128)(2,1)S(1)}, u32[]{:S(2)}, u32[]{:S(2)}) collective-permute-start(bf16[2,16,2048]{2,1,0:T(8,128)(2,1)S(1)} %collective-permute-done.41.refs_1_), channel_id=1, source_target_pairs={{0,1},{1,2},{2,3},{3,0},{4,5},{5,6},{6,7},{7,4},{8,9},{9,10},{10,1... | collective-permute-start | bytes 393224 | tf_op jit(solution)/shard_map/cond/branch_2_fun/ppermute | solution.py:250
  77.7 5.5 %collective-permute-start.43 = (bf16[2,16,2048]{2,1,0:T(8,128)(2,1)S(1)}, bf16[2,16,2048]{2,1,0:T(8,128)(2,1)S(1)}, u32[]{:S(2)}, u32[]{:S(2)}) collective-permute-start(bf16[2,16,2048]{2,1,0:T(8,128)(2,1)S(1)} %collective-permute-done.41.refs_1_), channel_id=1, source_target_pairs={{0,3},{1,0},{2,1},{3,2},{4,7},{5,4},{6,5},{7,6},{8,11},{9,8},{10,9... | collective-permute-start | bytes 393224 | tf_op jit(solution)/shard_map/cond/branch_2_fun/ppermute | solution.py:250
